TPU v7x, 32 devices: a whole 2x2x4 slice. The times are simulated.
32 devices in a mesh: group: 2 (over y), shard: 16 (over z, x, core).
Axes of the slice: x: 2, y: 2, z: 4, core: 2. Of those that a mesh axis runs over, the one named last changes fastest.
Arguments:
- features: bfloat16 [32768, 768], P('shard'), may hold values from -6 to 6
- seed_rows: int32 [8192], P(('group', 'shard')), parts along dimension 0, may hold values from 0 to 2047
- request_rows: int32 [32, 16, 2, 8], P(('group', 'shard')), parts along dimension 0, may hold values from 0 to 2047
- block_counts: int32 [32, 16], P(('group', 'shard')), parts along dimension 0, may hold values from 0 to 2, as said below
- tiles: bfloat16 [32, 32, 8, 128], P(('group', 'shard')), parts along dimension 0, may hold values from -0.5 to 0.5
- tile_seed_block: int32 [32, 32], P(('group', 'shard')), parts along dimension 0, may hold values from 0 to 1
- w_self: bfloat16 [768, 1024], replicated, may hold values from -0.21875 to 0.21875
- w_neigh: bfloat16 [768, 1024], replicated, may hold values from -0.21875 to 0.21875
- grad_out: bfloat16 [8192, 1024], P(('group', 'shard')), parts along dimension 0, may hold values from -0.09375 to 0.09375
Outputs:
- hidden: bfloat16 [8192, 1024], P(('group', 'shard')), parts along dimension 0
- grad_self: float32 [1536, 1024], P(('group', 'shard')), parts along dimension 0
- grad_neigh: float32 [1536, 1024], P(('group', 'shard')), parts along dimension 0
There are 2 independent parts, one for each index of `group`. A program takes and returns all parts, laid end to end along the dimension named above; an argument that names none is the same for every part. Nothing has to cross between parts.
Inputs may be any that keep to these rules, and one draw needn't show every extreme that they name: Trainer t pulls block_counts[t, o] blocks from owner o; request_rows beyond that count are padding and are not used. In every draw some owner gets 2 blocks from every trainer. `seed_rows`: row numbers within the trainer's own rows. `tile_seed_block`: seed block of a slot's tile.
All inputs are finite; a program needn't handle non-finite values.
Results may differ from a plain program's by a relative error of at most 0.0053.
Values may be sent and summed in bfloat16 or wider, within the bound.
A program may use at most 64 MiB of HBM per device.

v0:
```python
import jax
import jax.numpy as jnp
from jax import lax
from jax.sharding import PartitionSpec as P


def activate(values):
    return jax.nn.gelu(values, approximate=True)


def body(
    features,
    seed_rows,
    request_rows,
    block_counts,
    tiles,
    tile_seed_block,
    w_self,
    w_neigh,
    grad_out,
):
    requests = request_rows[0]
    slot_count = requests.shape[1]
    feature_width = features.shape[1]
    usable_slots = (
        jnp.arange(slot_count, dtype=jnp.int32)[None, :] < block_counts[0][:, None]
    ).astype(jnp.int32)
    wanted = lax.all_to_all(requests, "shard", split_axis=0, concat_axis=0, tiled=True)
    usable_mask = lax.all_to_all(usable_slots, "shard", split_axis=0, concat_axis=0, tiled=True)
    selected_blocks = features[wanted]
    answered = lax.all_to_all(
        jnp.where(
            usable_mask[:, :, None, None] > 0, selected_blocks, jnp.zeros((), features.dtype)
        ),
        "shard",
        split_axis=0,
        concat_axis=0,
        tiled=True,
    )
    neighbour_frontier = answered.reshape(-1, feature_width)
    messages = jnp.dot(neighbour_frontier, w_neigh, preferred_element_type=jnp.float32).astype(
        jnp.bfloat16
    )
    seed_count = seed_rows.shape[0]
    block_rows = tiles.shape[3]
    blocks = seed_count // block_rows
    select_blocks = tile_seed_block[0][:, None] == jnp.arange(blocks, dtype=jnp.int32)[None, :]
    adjacency_matrix = jnp.where(
        select_blocks[:, None, :, None], tiles[0][:, :, None, :], jnp.zeros((), tiles.dtype)
    ).reshape(-1, seed_count)
    neighbour = jnp.dot(adjacency_matrix.T, messages, preferred_element_type=jnp.float32)
    own_rows = features[seed_rows]
    summed = jnp.dot(own_rows, w_self, preferred_element_type=jnp.float32) + neighbour
    hidden = activate(summed).astype(jnp.bfloat16)
    _, pullback = jax.vjp(activate, summed)
    grad_pre = pullback(grad_out.astype(jnp.float32))[0].astype(jnp.bfloat16)
    columns = own_rows
    grad_self = lax.psum_scatter(
        jnp.dot(columns.T, grad_pre, preferred_element_type=jnp.float32),
        "shard",
        scatter_dimension=0,
        tiled=True,
    )
    grad_msg = jnp.dot(adjacency_matrix, grad_pre, preferred_element_type=jnp.float32).astype(
        jnp.bfloat16
    )
    columns = neighbour_frontier
    grad_neigh = lax.psum_scatter(
        jnp.dot(columns.T, grad_msg, preferred_element_type=jnp.float32),
        "shard",
        scatter_dimension=0,
        tiled=True,
    )
    return (hidden, grad_self, grad_neigh)


def solution(mesh):
    in_specs = (
        P("shard", None),
        P(("group", "shard")),
        P(("group", "shard"), None, None, None),
        P(("group", "shard"), None),
        P(("group", "shard"), None, None, None),
        P(("group", "shard"), None),
        P(),
        P(),
        P(("group", "shard"), None),
    )
    out_specs = (
        P(("group", "shard"), None),
        P(("group", "shard"), None),
        P(("group", "shard"), None),
    )
    return jax.shard_map(body, mesh=mesh, in_specs=in_specs, out_specs=out_specs, check_vma=False)
```

profile of v0, /device:TPU:0, one launch (start us, length us, event | category | flops | bytes accessed | tf_op | source)
XLA Modules:
  0.0 200.4 jit_solution(155039224530178891)
XLA Ops:
  7.2 1.5 compare_convert_fusion
  8.7 7.4 %all-to-all-start = ((s32[16,1,2]{2,1,0:T(1,128)}), s32[16,1,2]{2,1,0:T(1,128)S(1)}, u32[]{:S(2)}, u32[]{:S(2)}) async-start(s32[16,1,2]{2,1,0:T(1,128)} %compare_convert_fusion), calls=%async_computation | async-start | bytes 16384 | tf_op jit(solution)/shard_map/all_to_all | solution.py:29
  16.0 0.7 compare_select_fusion.1
  16.7 1.4 copy.20
  18.1 1.9 gather_fusion
  20.0 2.3 %all-to-all-done = s32[16,1,2]{2,1,0:T(1,128)S(1)} async-done(((s32[16,1,2]{2,1,0:T(1,128)}), s32[16,1,2]{2,1,0:T(1,128)S(1)}, u32[]{:S(2)}, u32[]{:S(2)}) %all-to-all-start) | async-done | bytes 160 | tf_op jit(solution)/shard_map/all_to_all | solution.py:29
  22.4 3.7 %all-to-all-start.1 = ((s32[16,2,8]{2,1,0:T(2,128)}), s32[16,2,8]{2,1,0:T(2,128)S(1)}, u32[]{:S(2)}, u32[]{:S(2)}) async-start(s32[16,2,8]{2,1,0:T(2,128)} %bitcast.4), calls=%async_computation.1 | async-start | bytes 32768 | tf_op jit(solution)/shard_map/all_to_all | solution.py:28
  26.1 0.1 copy.18
  26.2 0.1 copy.19
  26.3 6.3 %all-to-all-done.1 = s32[16,2,8]{2,1,0:T(2,128)S(1)} async-done(((s32[16,2,8]{2,1,0:T(2,128)}), s32[16,2,8]{2,1,0:T(2,128)S(1)}, u32[]{:S(2)}, u32[]{:S(2)}) %all-to-all-start.1) | async-done | bytes 1056 | tf_op jit(solution)/shard_map/all_to_all | solution.py:28
  32.6 0.1 reshape.100
  32.7 1.2 gather_fusion.1
  33.9 0.9 broadcast_select_fusion
  34.7 3.6 %all-to-all-start.2 = ((bf16[16,2,8,768]{3,2,1,0:T(8,128)(2,1)}), bf16[16,2,8,768]{3,2,1,0:T(8,128)(2,1)S(1)}, u32[]{:S(2)}, u32[]{:S(2)}) async-start(bf16[16,2,8,768]{3,2,1,0:T(8,128)(2,1)} %broadcast_select_fusion), calls=%async_computation.2 | async-start | bytes 786432 | tf_op jit(solution)/shard_map/all_to_all | solution.py:31
  38.4 0.1 iota_compare_fusion
  38.4 1.7 fusion.11
  40.1 3.1 %fusion.22 = f32[256,1024]{1,0:T(8,128)} fusion(bf16[256,768]{1,0:T(8,128)(2,1)} %gather_fusion, bf16[768,1024]{1,0:T(8,128)(2,1)} %param.15), kind=kOutput, calls=%fused_computation.36 | convolution fusion | flops 402653184 | bytes 3014656 | tf_op jit(solution)/shard_map/dot_general | solution.py:53
  43.2 7.2 %all-to-all-done.2 = bf16[16,2,8,768]{3,2,1,0:T(8,128)(2,1)S(1)} async-done(((bf16[16,2,8,768]{3,2,1,0:T(8,128)(2,1)}), bf16[16,2,8,768]{3,2,1,0:T(8,128)(2,1)S(1)}, u32[]{:S(2)}, u32[]{:S(2)}) %all-to-all-start.2) | async-done | bytes 393248 | tf_op jit(solution)/shard_map/all_to_all | solution.py:31
  50.5 3.8 %multiply_convert_fusion = (bf16[256,1024]{1,0:T(8,128)(2,1)}, f32[256,1024]{1,0:T(8,128)}) fusion(f32[256,1024]{1,0:T(8,128)} %fusion.22, bf16[256,768]{1,0:T(8,128)(2,1)S(1)} %bitcast.26, bf16[768,1024]{1,0:T(8,128)(2,1)} %param.16, bf16[32,8,2,128]{3,2,1,0:T(2,128)(2,1)} %fusion.11), kind=kOutput, calls=%fused_computation.20 | convolution fusion | flops 539754496 | bytes 4718592 | tf_op jit(solution)/shard_map/dot_general | solution.py:51
  54.3 4.5 %fusion = f32[768,1024]{1,0:T(8,128)} fusion(bf16[256,768]{1,0:T(8,128)(2,1)S(1)} %bitcast.27, bf16[32,8,2,128]{3,2,1,0:T(2,128)(2,1)} %fusion.11, bf16[256,1024]{1,0:T(8,128)(2,1)} %param.17, f32[256,1024]{1,0:T(8,128)} %get-tuple-element.4), kind=kOutput, calls=%fused_computation.9 | convolution fusion | flops 542638080 | bytes 5242880 | tf_op jit(solution)/shard_map/dot_general | solution.py:69
  58.8 0.9 copy-done.1
  59.8 4.2 %fusion.20 = f32[768,1024]{1,0:T(8,128)} fusion(bf16[256,768]{1,0:T(8,128)(2,1)S(1)} %copy-done.1, bf16[256,1024]{1,0:T(8,128)(2,1)} %param.17, f32[256,1024]{1,0:T(8,128)} %get-tuple-element.4), kind=kOutput, calls=%fused_computation.35 | convolution fusion | flops 408158208 | bytes 5111808 | tf_op jit(solution)/shard_map/dot_general | solution.py:59
  64.0 60.0 %reduce-scatter.5.cloned.1.call-done = f32[48,1024]{1,0:T(8,128)} async-done(((f32[768,1024]{1,0:T(8,128)}), f32[48,1024]{1,0:T(8,128)}) %reduce-scatter.5.cloned.1.call-update) | async-done | bytes 196624 | tf_op jit(solution)/shard_map/reduce_scatter | solution.py:68
  124.0 69.6 %reduce-scatter.3.cloned.1.call-done = f32[48,1024]{1,0:T(8,128)} async-done(((f32[768,1024]{1,0:T(8,128)}), f32[48,1024]{1,0:T(8,128)}) %reduce-scatter.3.cloned.1.call-update) | async-done | bytes 196624 | tf_op jit(solution)/shard_map/reduce_scatter | solution.py:58
  (13 shorter events, 0.2 us)
Async XLA Ops:
  7.2 10.9 %copy-start = (bf16[2048,768]{1,0:T(8,128)(2,1)S(1)}, bf16[2048,768]{1,0:T(8,128)(2,1)}, u32[]{:S(2)}) copy-start(bf16[2048,768]{1,0:T(8,128)(2,1)} %param.9) | copy-start | bytes 9437188
  8.7 13.7 %all-to-all-start = ((s32[16,1,2]{2,1,0:T(1,128)}), s32[16,1,2]{2,1,0:T(1,128)S(1)}, u32[]{:S(2)}, u32[]{:S(2)}) async-start(s32[16,1,2]{2,1,0:T(1,128)} %compare_convert_fusion), calls=%async_computation | async-start | bytes 16384 | tf_op jit(solution)/shard_map/all_to_all | solution.py:29
  22.4 10.2 %all-to-all-start.1 = ((s32[16,2,8]{2,1,0:T(2,128)}), s32[16,2,8]{2,1,0:T(2,128)S(1)}, u32[]{:S(2)}, u32[]{:S(2)}) async-start(s32[16,2,8]{2,1,0:T(2,128)} %bitcast.4), calls=%async_computation.1 | async-start | bytes 32768 | tf_op jit(solution)/shard_map/all_to_all | solution.py:28
  33.9 4.5 %copy-start.2 = (s32[1,32]{1,0:T(1,128)S(1)}, s32[1,32]{1,0:T(1,128)}, u32[]{:S(2)}) copy-start(s32[1,32]{1,0:T(1,128)} %param.14) | copy-start | bytes 388
  34.7 15.7 %all-to-all-start.2 = ((bf16[16,2,8,768]{3,2,1,0:T(8,128)(2,1)}), bf16[16,2,8,768]{3,2,1,0:T(8,128)(2,1)S(1)}, u32[]{:S(2)}, u32[]{:S(2)}) async-start(bf16[16,2,8,768]{3,2,1,0:T(8,128)(2,1)} %broadcast_select_fusion), calls=%async_computation.2 | async-start | bytes 786432 | tf_op jit(solution)/shard_map/all_to_all | solution.py:31
  38.3 85.7 %reduce-scatter.5.cloned.1.call-start = ((), (), s32[]{:S(2)}) async-start(), calls=%async_computation.6 | async-start | bytes 3342336 | tf_op jit(solution)/shard_map/reduce_scatter | solution.py:68
  58.8 1.0 copy-start.1
  58.8 134.8 %reduce-scatter.3.cloned.1.call-start = ((), (), s32[]{:S(2)}) async-start(), calls=%async_computation.5 | async-start | bytes 3342336 | tf_op jit(solution)/shard_map/reduce_scatter | solution.py:58
Sparse Core Ops, SparseCore 0:
  58.9 65.0 reduce-scatter.4
  128.3 65.1 reduce-scatter.2
where the time goes:
time: 201 us; the launch traced here: 200 us
  waiting for transfers between devices  145 us (72%)
  matrix products  15.6 us (8%)
  starting transfers between devices  14.7 us (7%)
  between operations  14.1 us (7%)
  local copies, waits for them, and re-layouts  5.72 us (3%)
  other arithmetic  4.81 us (2%)
    reduce_scatter x1, waiting for transfers between devices, body(): lax.psum_scatter(jnp.dot(columns.T, grad_pre, preferred_element_type=jnp....  69.6 us
    reduce_scatter x1, waiting for transfers between devices, body(): lax.psum_scatter(jnp.dot(columns.T, grad_msg, preferred_element_type=jnp....  60 us
    all_to_all x1, starting transfers between devices, body(): lax.all_to_all(usable_slots, 'shard', split_axis=0, concat_axis=0, tiled=...  7.36 us
    all_to_all x1, waiting for transfers between devices, body(): lax.all_to_all(jnp.where(usable_mask[:, :, None, None] > 0, selected_bloc...  7.23 us
    all_to_all x1, waiting for transfers between devices, body(): lax.all_to_all(requests, 'shard', split_axis=0, concat_axis=0, tiled=True)  6.31 us
    dot_general x1, matrix products, body(): jnp.dot(columns.T, grad_msg, preferred_element_type=jnp.float32)  4.47 us
    dot_general x1, matrix products, body(): jnp.dot(columns.T, grad_pre, preferred_element_type=jnp.float32)  4.2 us
  transfers between devices with their start and end apart: 5, of which 5 were waited for; matrix products, arithmetic and copies ran while one was open for 7% of the time, Pallas kernels for 0%

commit v1 on v0

v1 whole, which is shorter than its diff:
```python
import functools

import jax
import jax.numpy as jnp
from jax import lax
from jax.experimental import pallas as pl
from jax.experimental.pallas import tpu as pltpu
from jax.sharding import PartitionSpec as P

MESH = pl.DeviceIdType.MESH
BF16 = jnp.bfloat16
F32 = jnp.float32
LANES = 128
NZ, NX, NC = 4, 2, 2


def activate(values):
    return jax.nn.gelu(values, approximate=True)


def generic_body(
    features,
    seed_rows,
    request_rows,
    block_counts,
    tiles,
    tile_seed_block,
    w_self,
    w_neigh,
    grad_out,
):
    requests = request_rows[0]
    slot_count = requests.shape[1]
    feature_width = features.shape[1]
    usable = jnp.arange(slot_count, dtype=jnp.int32)[None, :] < block_counts[0][:, None]
    wanted = lax.all_to_all(
        jnp.where(usable[:, :, None], requests, -1), "shard", split_axis=0, concat_axis=0, tiled=True
    )
    selected_blocks = features[jnp.maximum(wanted, 0)]
    answered = lax.all_to_all(
        jnp.where(wanted[..., None] >= 0, selected_blocks, jnp.zeros((), features.dtype)),
        "shard",
        split_axis=0,
        concat_axis=0,
        tiled=True,
    )
    neighbour_frontier = answered.reshape(-1, feature_width)
    messages = jnp.dot(neighbour_frontier, w_neigh, preferred_element_type=F32).astype(BF16)
    seed_count = seed_rows.shape[0]
    block_rows = tiles.shape[3]
    blocks = seed_count // block_rows
    select_blocks = tile_seed_block[0][:, None] == jnp.arange(blocks, dtype=jnp.int32)[None, :]
    adjacency_matrix = jnp.where(
        select_blocks[:, None, :, None], tiles[0][:, :, None, :], jnp.zeros((), tiles.dtype)
    ).reshape(-1, seed_count)
    neighbour = jnp.dot(adjacency_matrix.T, messages, preferred_element_type=F32)
    own_rows = features[seed_rows]
    summed = jnp.dot(own_rows, w_self, preferred_element_type=F32) + neighbour
    hidden = activate(summed).astype(BF16)
    _, pullback = jax.vjp(activate, summed)
    grad_pre = pullback(grad_out.astype(F32))[0].astype(BF16)
    grad_self = lax.psum_scatter(
        jnp.dot(own_rows.T, grad_pre, preferred_element_type=F32),
        "shard",
        scatter_dimension=0,
        tiled=True,
    )
    grad_msg = jnp.dot(adjacency_matrix, grad_pre, preferred_element_type=F32).astype(BF16)
    grad_neigh = lax.psum_scatter(
        jnp.dot(neighbour_frontier.T, grad_msg, preferred_element_type=F32),
        "shard",
        scatter_dimension=0,
        tiled=True,
    )
    return (hidden, grad_self, grad_neigh)


def down_rows(row):
    return jnp.broadcast_to(row, (LANES, LANES)).T


def put_one_hot(oh, row, base, count):
    ids = down_rows(row)
    lane = lax.broadcasted_iota(jnp.int32, (LANES, LANES), 1)
    for c in range(count // LANES):
        oh[base : base + LANES, c * LANES : (c + 1) * LANES] = (
            (ids == lane + c * LANES).astype(F32).astype(BF16)
        )


def kernel(
    req_ref,
    ids_ref,
    tiles_ref,
    feat_hbm,
    ws_hbm,
    wn_hbm,
    go_hbm,
    hid_hbm,
    gs_ref,
    gn_ref,
    feat,
    ws,
    wn,
    gout,
    oh,
    reqs,
    ans,
    rows,
    adj,
    adjt,
    s,
    hid,
    rrows,
    at,
    bcat,
    bsend,
    xsend,
    xrecv,
    gk,
    zsend,
    zrecv,
    lsem,
    hsem,
    rq_s,
    rq_r,
    fr_s,
    fr_r,
    a_s,
    a_r,
    b_s,
    b_r,
    x_s,
    x_r,
    z_s,
    z_r,
):
    n = NZ * NX * NC
    me = lax.axis_index("shard")
    z, x, core = me // (NX * NC), (me // NC) % NX, me % NC
    half_n = n // 2
    near, far = me // half_n, 1 - me // half_n
    node_count, width = feat.shape
    per = ans.shape[2]
    nq, wq = hid.shape[0], hid.shape[2]
    seeds = hid.shape[1]

    def dev(zz, xx, cc):
        return {"shard": zz * (NX * NC) + xx * NC + cc}

    def z_xor(k):
        return (z, z + 1 - 2 * (z % 2), lax.rem(z + 2, NZ), NZ - 1 - z)[k]

    loads = [
        pltpu.make_async_copy(src, dst, lsem.at[i])
        for i, (src, dst) in enumerate(
            ((feat_hbm, feat), (ws_hbm, ws), (wn_hbm, wn), (go_hbm, gout))
        )
    ]
    for load in loads:
        load.start()
    barrier = pltpu.get_barrier_semaphore()
    others = [lax.rem(me + k, n) for k in range(1, n)]
    for other in others:
        pl.semaphore_signal(barrier, inc=1, device_id={"shard": other}, device_id_type=MESH)
    pl.semaphore_wait(barrier, n - 1)

    ask = []
    for k, owner in enumerate(others):
        ask.append(
            pltpu.make_async_remote_copy(
                src_ref=req_ref.at[owner],
                dst_ref=reqs.at[me],
                send_sem=rq_s.at[k],
                recv_sem=rq_r.at[me],
                device_id={"shard": owner},
                device_id_type=MESH,
            )
        )
        ask[-1].start()
    reqs[me] = req_ref[me]

    for h in range(seeds // LANES):
        put_one_hot(oh, ids_ref[h], h * LANES, node_count)
    loads[0].wait()
    for h in range(seeds // LANES):
        rows[h] = jnp.dot(
            oh[h * LANES : (h + 1) * LANES, :], feat[...], preferred_element_type=F32
        ).astype(BF16)

    lane = lax.broadcasted_iota(jnp.int32, (1, LANES), 1)
    answer = []
    for step, h in enumerate((far, near)):
        wanted = jnp.zeros((1, LANES), jnp.int32)
        for j in range(half_n):
            src = h * half_n + j

            @pl.when(src != me)
            def _():
                pltpu.make_async_remote_copy(
                    src_ref=reqs.at[src],
                    dst_ref=reqs.at[src],
                    send_sem=rq_s.at[0],
                    recv_sem=rq_r.at[src],
                    device_id={"shard": others[0]},
                    device_id_type=MESH,
                ).wait_recv()

            wanted = jnp.where(lane // per == j, reqs[src], wanted)
        put_one_hot(oh, wanted, 0, node_count)
        ans[h] = (
            jnp.dot(oh[0:LANES, :], feat[...], preferred_element_type=F32)
            .astype(BF16)
            .reshape(half_n, per, width)
        )
        mine = rows.at[2 + near, pl.ds(pl.multiple_of((me % half_n) * per, per), per)]
        for j in range(half_n):
            slot = lax.rem(me + j, half_n)
            dst = h * half_n + slot
            copy = pltpu.make_async_remote_copy(
                src_ref=ans.at[h, slot],
                dst_ref=mine,
                send_sem=fr_s.at[step, j],
                recv_sem=fr_r.at[me],
                device_id={"shard": dst},
                device_id_type=MESH,
            )
            if step == 1 and j == 0:
                own = pltpu.make_async_copy(ans.at[h, slot], mine, hsem.at[nq])
                own.start()
            else:
                copy.start()
                answer.append(copy)

    for h in range(2):
        seed_block = down_rows(ids_ref[2 + h])
        tile = tiles_ref[h * LANES : (h + 1) * LANES, :].astype(F32)
        for b in range(seeds // LANES):
            part = jnp.where(seed_block == b, tile, 0.0)
            adj[h * LANES : (h + 1) * LANES, b * LANES : (b + 1) * LANES] = part.astype(BF16)
            adjt[h, b * LANES : (b + 1) * LANES, :] = part.T.astype(BF16)
    loads[1].wait()
    own_rows = rows[0:2].reshape(seeds, width)
    for q in range(nq):
        s[q] = jnp.dot(own_rows, ws[:, q * wq : (q + 1) * wq], preferred_element_type=F32)
    loads[2].wait()
    loads[3].wait()

    def wait_rows(h, skip_me):
        for j in range(half_n):
            owner = h * half_n + j

            def wait():
                where = rows.at[2 + h, pl.ds(j * per, per)]
                pltpu.make_async_remote_copy(
                    src_ref=where,
                    dst_ref=where,
                    send_sem=fr_s.at[0, 0],
                    recv_sem=fr_r.at[owner],
                    device_id={"shard": others[0]},
                    device_id_type=MESH,
                ).wait_recv()

            if skip_me:
                pl.when(owner != me)(wait)
            else:
                wait()

    own.wait()
    wait_rows(near, True)
    for q in range(nq):
        msg = jnp.dot(
            rows[2 + near], wn[:, q * wq : (q + 1) * wq], preferred_element_type=F32
        ).astype(BF16)
        s[q] += jnp.dot(adjt[near], msg, preferred_element_type=F32)
    wait_rows(far, False)

    sibling = dev(z, x, 1 - core)
    trade_a = pltpu.make_async_remote_copy(
        src_ref=rows.at[pl.ds(2 * (1 - core), 2)],
        dst_ref=rrows,
        send_sem=a_s,
        recv_sem=a_r,
        device_id=sibling,
        device_id_type=MESH,
    )
    trade_a.start()
    trade_b, writes, xcopies, zcopies = [], [], [], []

    def seed_part(q):
        cols = slice(q * wq, (q + 1) * wq)
        msg = jnp.dot(rows[2 + far], wn[:, cols], preferred_element_type=F32).astype(BF16)
        v = s[q] + jnp.dot(adjt[far], msg, preferred_element_type=F32)
        c0 = 0.7978845608028654
        v2 = v * v
        t = jnp.tanh(c0 * v * (1.0 + 0.044715 * v2))
        cdf = 0.5 * (1.0 + t)
        hid[q] = (v * cdf).astype(BF16)
        slope = cdf + 0.5 * v * (1.0 - t * t) * (c0 * (1.0 + (3 * 0.044715) * v2))
        gp = (gout[:, cols].astype(F32) * slope).astype(BF16)
        gm = jnp.dot(adj[...], gp, preferred_element_type=F32).astype(BF16)

        @pl.when(core == 0)
        def _():
            bcat[q, 0:seeds, :] = gp
            bsend[q] = gm

        @pl.when(core != 0)
        def _():
            bcat[q, 0:seeds, :] = gm
            bsend[q] = gp

        copy = pltpu.make_async_remote_copy(
            src_ref=bsend.at[q],
            dst_ref=bcat.at[q, pl.ds(seeds, seeds)],
            send_sem=b_s.at[q],
            recv_sem=b_r.at[q],
            device_id=sibling,
            device_id_type=MESH,
        )
        copy.start()
        trade_b.append(copy)
        write = pltpu.make_async_copy(hid.at[q], hid_hbm.at[:, pl.ds(q * wq, wq)], hsem.at[q])
        write.start()
        writes.append(write)

    chip_rows = width // (NZ * NX)

    def put_transposed(values, at_col):
        turned = values.T
        for zz in range(NZ):
            for xx in range(NX):
                start = (zz * NX + xx) * chip_rows
                at[xx, zz * chip_rows : (zz + 1) * chip_rows, at_col : at_col + seeds] = turned[
                    start : start + chip_rows, :
                ]

    peer = dev(z, 1 - x, core)

    def x_part(q):
        trade_b[q].wait_recv()
        xsend[q] = (
            jnp.dot(at[1 - x], bcat[q], preferred_element_type=F32)
            .astype(BF16)
            .reshape(NZ, chip_rows, wq)
        )
        for k in range(NZ - 1, -1, -1):
            zb = z_xor(k)
            copy = pltpu.make_async_remote_copy(
                src_ref=xsend.at[q, zb],
                dst_ref=xrecv.at[q, zb],
                send_sem=x_s.at[q, k],
                recv_sem=x_r.at[q, k],
                device_id=peer,
                device_id_type=MESH,
            )
            copy.start()
            xcopies.append(copy)
        gk[q] = jnp.dot(at[x], bcat[q], preferred_element_type=F32).reshape(NZ, chip_rows, wq)

    def z_part(q):
        for k in range(NZ - 1, -1, -1):
            zb = z_xor(k)
            xcopies[q * NZ + NZ - 1 - k].wait_recv()
            total = gk[q, zb] + xrecv[q, zb].astype(F32)
            zsend[q, zb] = total.astype(BF16).reshape(NC, chip_rows // NC, wq)
            for i in range(NC):
                cc = 1 - core if i == 0 else core
                if k == 0 and i == 1:
                    zrecv[q, core, z] = zsend[q, z, core]
                    continue
                copy = pltpu.make_async_remote_copy(
                    src_ref=zsend.at[q, zb, cc],
                    dst_ref=zrecv.at[q, core, z],
                    send_sem=z_s.at[q, k, i],
                    recv_sem=z_r.at[q, core, z],
                    device_id=dev(zb, x, cc),
                    device_id_type=MESH,
                )
                copy.start()
                zcopies.append(copy)

    def last_part(q):
        for i in range(NC):
            for k in range(NZ):
                if i == 0 and k == 0:
                    continue
                g = core if i == 0 else 1 - core
                where = zrecv.at[q, g, z_xor(k)]
                pltpu.make_async_remote_copy(
                    src_ref=where,
                    dst_ref=where,
                    send_sem=z_s.at[0, 0, 0],
                    recv_sem=z_r.at[q, g, z_xor(k)],
                    device_id=sibling,
                    device_id_type=MESH,
                ).wait_recv()
        for g, out in enumerate((gs_ref, gn_ref)):
            parts = zrecv[q, g].astype(F32)
            out[:, q * wq : (q + 1) * wq] = (parts[0] + parts[1]) + (parts[2] + parts[3])

    seed_part(0)
    put_transposed(rows[pl.ds(2 * core, 2)].reshape(seeds, width), 0)
    seed_part(1)
    trade_a.wait_recv()
    put_transposed(rrows[...].reshape(seeds, width), seeds)
    x_part(0)
    for q in range(2, nq):
        seed_part(q)
        x_part(q - 1)
    x_part(nq - 1)
    for q in range(nq):
        z_part(q)
    for q in range(nq):
        last_part(q)
    for copy in ask + answer + [trade_a] + trade_b + xcopies + zcopies:
        copy.wait_send()
    for write in writes:
        write.wait()


def kernel_body(
    features,
    seed_rows,
    request_rows,
    block_counts,
    tiles,
    tile_seed_block,
    w_self,
    w_neigh,
    grad_out,
):
    n, cap, block = request_rows.shape[1:]
    per = cap * block
    node_count, width = features.shape
    seeds, hidden_width = grad_out.shape
    usable = jnp.arange(cap, dtype=jnp.int32)[None, :] < block_counts[0][:, None]
    wanted = jnp.where(usable[:, :, None], request_rows[0], -1).reshape(n, 1, per)
    wanted = jnp.tile(wanted, (1, 1, LANES // per))
    ids = jnp.concatenate([seed_rows, jnp.repeat(tile_seed_block[0], block)]).reshape(4, 1, LANES)
    nq = 4
    wq = hidden_width // nq
    chip_rows = width // (NZ * NX)
    out_rows = width // n
    vmem = pl.BlockSpec(memory_space=pltpu.VMEM)
    hbm = pl.BlockSpec(memory_space=pl.ANY)
    dma = pltpu.SemaphoreType.DMA
    return pl.pallas_call(
        kernel,
        out_shape=(
            jax.ShapeDtypeStruct((seeds, hidden_width), BF16),
            jax.ShapeDtypeStruct((out_rows, hidden_width), F32),
            jax.ShapeDtypeStruct((out_rows, hidden_width), F32),
        ),
        in_specs=[vmem] * 3 + [hbm] * 4,
        out_specs=(hbm, vmem, vmem),
        scratch_shapes=[
            pltpu.VMEM((node_count, width), BF16),
            pltpu.VMEM((width, hidden_width), BF16),
            pltpu.VMEM((width, hidden_width), BF16),
            pltpu.VMEM((seeds, hidden_width), BF16),
            pltpu.VMEM((seeds, node_count), BF16),
            pltpu.VMEM((n, 1, LANES), jnp.int32),
            pltpu.VMEM((2, n // 2, per, width), BF16),
            pltpu.VMEM((4, LANES, width), BF16),
            pltpu.VMEM((seeds, seeds), BF16),
            pltpu.VMEM((2, seeds, LANES), BF16),
            pltpu.VMEM((nq, seeds, wq), F32),
            pltpu.VMEM((nq, seeds, wq), BF16),
            pltpu.VMEM((2, LANES, width), BF16),
            pltpu.VMEM((NX, NZ * chip_rows, 2 * seeds), BF16),
            pltpu.VMEM((nq, 2 * seeds, wq), BF16),
            pltpu.VMEM((nq, seeds, wq), BF16),
            pltpu.VMEM((nq, NZ, chip_rows, wq), BF16),
            pltpu.VMEM((nq, NZ, chip_rows, wq), BF16),
            pltpu.VMEM((nq, NZ, chip_rows, wq), F32),
            pltpu.VMEM((nq, NZ, NC, out_rows, wq), BF16),
            pltpu.VMEM((nq, NC, NZ, out_rows, wq), BF16),
            dma((4,)),
            dma((nq + 1,)),
            dma((n - 1,)),
            dma((n,)),
            dma((2, n // 2)),
            dma((n,)),
            dma,
            dma,
            dma((nq,)),
            dma((nq,)),
            dma((nq, NZ)),
            dma((nq, NZ)),
            dma((nq, NZ, NC)),
            dma((nq, NC, NZ)),
        ],
        compiler_params=pltpu.CompilerParams(
            collective_id=0, has_side_effects=True, vmem_limit_bytes=48 * 1024 * 1024
        ),
        name="layer_step",
    )(
        wanted,
        ids,
        tiles.reshape(-1, tiles.shape[3]),
        features,
        w_self,
        w_neigh,
        grad_out,
    )


def solution(mesh):
    in_specs = (
        P("shard", None),
        P(("group", "shard")),
        P(("group", "shard"), None, None, None),
        P(("group", "shard"), None),
        P(("group", "shard"), None, None, None),
        P(("group", "shard"), None),
        P(),
        P(),
        P(("group", "shard"), None),
    )
    out_specs = (
        P(("group", "shard"), None),
        P(("group", "shard"), None),
        P(("group", "shard"), None),
    )
    body = kernel_body if mesh.shape["shard"] == NZ * NX * NC else generic_body
    return jax.shard_map(body, mesh=mesh, in_specs=in_specs, out_specs=out_specs, check_vma=False)
```

time: 201 us -> 58.7 us (0.29)
  waiting for transfers between devices: 145 us -> 0 us
  Pallas kernels: 0 us -> 46.6 us
  matrix products: 15.6 us -> 0 us
  starting transfers between devices: 14.7 us -> 0 us
  between operations: 14.1 us -> 0.66 us
  local copies, waits for them, and re-layouts: 5.72 us -> 7.76 us
    reduce_scatter x2 -> x0, waiting for transfers between devices: 130 us -> none  [the longest x1 69.6 us: body(): lax.psum_scatter(jnp.dot(columns.T, grad_pre, preferred_element_type=jnp....]
    pallas_call x0 -> x1, Pallas kernels: none -> 46.6 us  [kernel_body(): pl.pallas_call(kernel, out_shape=(jax.ShapeDtypeStruct((seeds, hidden_wid...]
    all_to_all x3 -> x0, waiting for transfers between devices: 15.9 us -> none  [the longest x1 7.23 us: body(): lax.all_to_all(jnp.where(usable_mask[:, :, None, None] > 0, selected_bloc...]
    dot_general x4 -> x0, matrix products: 15.6 us -> none  [the longest x1 4.47 us: body(): jnp.dot(columns.T, grad_msg, preferred_element_type=jnp.float32)]
    all_to_all x3 -> x0, starting transfers between devices: 14.6 us -> none  [the longest x1 7.36 us: body(): lax.all_to_all(usable_slots, 'shard', split_axis=0, concat_axis=0, tiled=...]
    unnamed x7 -> x12, local copies, waits for them, and re-layouts: 2.31 us -> 7.35 us
    gather x2 -> x0, local copies, waits for them, and re-layouts: 3.13 us -> none  [the longest x1 1.94 us: body(): own_rows = features[seed_rows]]
  transfers between devices with their start and end apart: 5 -> 0, of which waited for: 5 -> 0; matrix products, arithmetic and copies ran while one was open for 7% -> 0% of each run, Pallas kernels for 0% -> 0%
where the time goes in v1:
time: 58.7 us; the launch traced here: 58.3 us
  Pallas kernels  46.6 us (79%)
  local copies, waits for them, and re-layouts  7.76 us (13%)
  other arithmetic  3.36 us (6%)
  between operations  0.66 us (1%)
    pallas_call x1, Pallas kernels, kernel_body(): pl.pallas_call(kernel, out_shape=(jax.ShapeDtypeStruct((seeds, hidden_wid...  46.6 us
    unnamed x12, local copies, waits for them, and re-layouts  7.35 us
    unnamed x1, other arithmetic  1.32 us

profile of v1, /device:TPU:0, one launch (start us, length us, event | category | flops | bytes accessed | tf_op | source)
XLA Modules:
  0.0 58.3 jit_solution(8205393923594927670)
XLA Ops:
  0.6 0.5 broadcast.29
  1.1 1.3 %reduce.3 = s32[32]{0:T(128)S(1)} reduce(s32[1,32]{1,0:T(1,128)} %param.14, s32[]{:T(128)} %broadcast.29), dimensions={0}, to_apply=%param.14.reduce_sub_computation.3 | reduce | bytes 260 | tf_op args[5]
  2.5 0.7 %iota_compare_fusion = pred[16,2]{0,1:T(4,128)(4,1)S(1)} fusion(s32[16]{0:T(128)} %bitcast.11), kind=kLoop, calls=%fused_computation.2 | loop fusion | flops 32 | bytes 96 | tf_op jit(solution)/shard_map/lt | solution.py:437
  3.1 0.1 broadcast_in_dim.26
  3.2 0.7 %bitcast_select_fusion = s32[16,16]{0,1:T(8,128)S(1)} fusion(s32[1,16,2,8]{1,3,2,0:T(8,128)} %param.11, pred[16,2]{0,1:T(4,128)(4,1)S(1)} %iota_compare_fusion), kind=kLoop, calls=%fused_computation | loop fusion | flops 256 | bytes 2080 | tf_op jit(solution)/shard_map/jit(_where)/select_n | solution.py:438
  3.9 0.1 copy.13
  4.0 0.1 broadcast_in_dim.27
  4.0 0.1 broadcast_in_dim.28
  4.1 0.7 %pad_add_fusion.ids_ref = s32[4,1,128]{2,1,0:T(1,128)S(1)} fusion(s32[2,1,128]{2,1,0:T(1,128)S(1)} %bitcast.9, s32[2,1,128]{2,1,0:T(1,128)} %bitcast.10), kind=kLoop, calls=%fused_computation.1 | loop fusion | flops 512 | bytes 4096 | tf_op jit(solution)/shard_map/concatenate | solution.py:440
  4.8 0.1 tile.9.req_ref
  4.9 0.0 copy-start
  4.9 1.4 %copy-done = bf16[768,1024]{1,0:T(8,128)(2,1)S(1)} copy-done((bf16[768,1024]{1,0:T(8,128)(2,1)S(1)}, bf16[768,1024]{1,0:T(8,128)(2,1)}, u32[]{:S(2)}) %copy-start) | copy-done | bytes 1572888
  6.3 0.0 copy-start.1
  6.3 1.4 %copy-done.1 = bf16[768,1024]{1,0:T(8,128)(2,1)S(1)} copy-done((bf16[768,1024]{1,0:T(8,128)(2,1)S(1)}, bf16[768,1024]{1,0:T(8,128)(2,1)}, u32[]{:S(2)}) %copy-start.1) | copy-done | bytes 1572888
  7.7 0.0 copy-start.2
  7.7 1.0 %copy-done.2 = bf16[256,1024]{1,0:T(8,128)(2,1)S(1)} copy-done((bf16[256,1024]{1,0:T(8,128)(2,1)S(1)}, bf16[256,1024]{1,0:T(8,128)(2,1)}, u32[]{:S(2)}) %copy-start.2) | copy-done | bytes 524312
  8.8 0.0 copy-start.3
  8.8 0.8 %copy-done.3 = bf16[1,32,8,128]{3,2,1,0:T(8,128)(2,1)S(1)} copy-done((bf16[1,32,8,128]{3,2,1,0:T(8,128)(2,1)S(1)}, bf16[1,32,8,128]{3,2,1,0:T(8,128)(2,1)}, u32[]{:S(2)}) %copy-start.3) | copy-done | bytes 65560
  9.6 46.6 %layer_step.1 = (bf16[256,1024]{1,0:T(8,128)(2,1)S(1)}, f32[48,1024]{1,0:T(8,128)S(1)}, f32[48,1024]{1,0:T(8,128)S(1)}) custom-call(s32[16,1,128]{2,1,0:T(1,128)S(1)} %tile.9.req_ref, s32[4,1,128]{2,1,0:T(1,128)S(1)} %pad_add_fusion.ids_ref, bf16[256,128]{1,0:T(8,128)(2,1)S(1)} %bitcast.8, bf16[2048,768]{1,0:T(8,128)(2,1)} %feat_hbm.1, ...), custom_call_target="tpu_custom_call" | custom-call | tf_op jit(solution)/shard_map/layer_step/pallas_call | solution.py:448
  56.2 0.8 %copy.18 = bf16[256,1024]{1,0:T(8,128)(2,1)} copy(bf16[256,1024]{1,0:T(8,128)(2,1)S(1)} %get-tuple-element.6) | data formatting | bytes 1048576
  57.0 0.7 %copy.19 = f32[48,1024]{1,0:T(8,128)} copy(f32[48,1024]{1,0:T(8,128)S(1)} %get-tuple-element.7) | data formatting | bytes 393216
  57.7 0.7 %copy.20 = f32[48,1024]{1,0:T(8,128)} copy(f32[48,1024]{1,0:T(8,128)S(1)} %get-tuple-element.8) | data formatting | bytes 393216
  (1 shorter events, 0.0 us)
Async XLA Ops:
  4.9 1.4 %copy-start = (bf16[768,1024]{1,0:T(8,128)(2,1)S(1)}, bf16[768,1024]{1,0:T(8,128)(2,1)}, u32[]{:S(2)}) copy-start(bf16[768,1024]{1,0:T(8,128)(2,1)} %ws_hbm.1) | copy-start | bytes 4718596
  6.3 1.4 %copy-start.1 = (bf16[768,1024]{1,0:T(8,128)(2,1)S(1)}, bf16[768,1024]{1,0:T(8,128)(2,1)}, u32[]{:S(2)}) copy-start(bf16[768,1024]{1,0:T(8,128)(2,1)} %wn_hbm.1) | copy-start | bytes 4718596
  7.7 1.0 %copy-start.2 = (bf16[256,1024]{1,0:T(8,128)(2,1)S(1)}, bf16[256,1024]{1,0:T(8,128)(2,1)}, u32[]{:S(2)}) copy-start(bf16[256,1024]{1,0:T(8,128)(2,1)} %go_hbm.1) | copy-start | bytes 1572868
  8.8 0.8 %copy-start.3 = (bf16[1,32,8,128]{3,2,1,0:T(8,128)(2,1)S(1)}, bf16[1,32,8,128]{3,2,1,0:T(8,128)(2,1)}, u32[]{:S(2)}) copy-start(bf16[1,32,8,128]{3,2,1,0:T(8,128)(2,1)} %param.13) | copy-start | bytes 196612

commit v2 on v1

--- a/solution.py
+++ b/solution.py
@@ -79,8 +79,7 @@
     return jnp.broadcast_to(row, (LANES, LANES)).T
 
 
-def put_one_hot(oh, row, base, count):
-    ids = down_rows(row)
+def put_one_hot(oh, ids, base, count):
     lane = lax.broadcasted_iota(jnp.int32, (LANES, LANES), 1)
     for c in range(count // LANES):
         oh[base : base + LANES, c * LANES : (c + 1) * LANES] = (
@@ -89,8 +88,10 @@
 
 
 def kernel(
-    req_ref,
-    ids_ref,
+    counts_ref,
+    block_ref,
+    wanted_ref,
+    seeds_ref,
     tiles_ref,
     feat_hbm,
     ws_hbm,
@@ -104,9 +105,12 @@
     wn,
     gout,
     oh,
+    turn,
+    req_ref,
     reqs,
     ans,
     rows,
+    adj32,
     adj,
     adjt,
     s,
@@ -163,6 +167,14 @@
     others = [lax.rem(me + k, n) for k in range(1, n)]
     for other in others:
         pl.semaphore_signal(barrier, inc=1, device_id={"shard": other}, device_id_type=MESH)
+    cap, block = wanted_ref.shape[:2]
+    for j in range(cap):
+        turn[j * block : (j + 1) * block, 0:n] = jnp.where(
+            j < counts_ref[...], wanted_ref[j], -1
+        )
+    turned = turn[...].T
+    for owner in range(n):
+        req_ref[owner] = turned[owner : owner + 1, :]
     pl.semaphore_wait(barrier, n - 1)
 
     ask = []
@@ -181,17 +193,15 @@
     reqs[me] = req_ref[me]
 
     for h in range(seeds // LANES):
-        put_one_hot(oh, ids_ref[h], h * LANES, node_count)
+        put_one_hot(oh, down_rows(seeds_ref[h : h + 1, :]), h * LANES, node_count)
     loads[0].wait()
     for h in range(seeds // LANES):
         rows[h] = jnp.dot(
             oh[h * LANES : (h + 1) * LANES, :], feat[...], preferred_element_type=F32
         ).astype(BF16)
 
-    lane = lax.broadcasted_iota(jnp.int32, (1, LANES), 1)
     answer = []
     for step, h in enumerate((far, near)):
-        wanted = jnp.zeros((1, LANES), jnp.int32)
         for j in range(half_n):
             src = h * half_n + j
 
@@ -205,9 +215,12 @@
                     device_id={"shard": others[0]},
                     device_id_type=MESH,
                 ).wait_recv()
-
-            wanted = jnp.where(lane // per == j, reqs[src], wanted)
-        put_one_hot(oh, wanted, 0, node_count)
+            turn[j : j + 1, :] = reqs[src]
+        turned = turn[...].T
+        wanted = [
+            jnp.broadcast_to(turned[0:per, j : j + 1], (per, LANES)) for j in range(half_n)
+        ]
+        put_one_hot(oh, jnp.concatenate(wanted, axis=0), 0, node_count)
         ans[h] = (
             jnp.dot(oh[0:LANES, :], feat[...], preferred_element_type=F32)
             .astype(BF16)
@@ -217,6 +230,10 @@
         for j in range(half_n):
             slot = lax.rem(me + j, half_n)
             dst = h * half_n + slot
+            if step == 1 and j == 0:
+                own = pltpu.make_async_copy(ans.at[h, slot], mine, hsem.at[nq])
+                own.start()
+                continue
             copy = pltpu.make_async_remote_copy(
                 src_ref=ans.at[h, slot],
                 dst_ref=mine,
@@ -225,20 +242,18 @@
                 device_id={"shard": dst},
                 device_id_type=MESH,
             )
-            if step == 1 and j == 0:
-                own = pltpu.make_async_copy(ans.at[h, slot], mine, hsem.at[nq])
-                own.start()
-            else:
-                copy.start()
-                answer.append(copy)
-
+            copy.start()
+            answer.append(copy)
+
+    for slot in range(tiles_ref.shape[0]):
+        tile = tiles_ref[slot].astype(F32)
+        for b in range(seeds // LANES):
+            adj32[slot * block : (slot + 1) * block, b * LANES : (b + 1) * LANES] = jnp.where(
+                block_ref[0, slot] == b, tile, 0.0
+            )
+    adj[...] = adj32[...].astype(BF16)
     for h in range(2):
-        seed_block = down_rows(ids_ref[2 + h])
-        tile = tiles_ref[h * LANES : (h + 1) * LANES, :].astype(F32)
-        for b in range(seeds // LANES):
-            part = jnp.where(seed_block == b, tile, 0.0)
-            adj[h * LANES : (h + 1) * LANES, b * LANES : (b + 1) * LANES] = part.astype(BF16)
-            adjt[h, b * LANES : (b + 1) * LANES, :] = part.T.astype(BF16)
+        adjt[h] = adj32[h * LANES : (h + 1) * LANES, :].T.astype(BF16)
     loads[1].wait()
     own_rows = rows[0:2].reshape(seeds, width)
     for q in range(nq):
@@ -434,25 +449,22 @@
     per = cap * block
     node_count, width = features.shape
     seeds, hidden_width = grad_out.shape
-    usable = jnp.arange(cap, dtype=jnp.int32)[None, :] < block_counts[0][:, None]
-    wanted = jnp.where(usable[:, :, None], request_rows[0], -1).reshape(n, 1, per)
-    wanted = jnp.tile(wanted, (1, 1, LANES // per))
-    ids = jnp.concatenate([seed_rows, jnp.repeat(tile_seed_block[0], block)]).reshape(4, 1, LANES)
     nq = 4
     wq = hidden_width // nq
     chip_rows = width // (NZ * NX)
     out_rows = width // n
     vmem = pl.BlockSpec(memory_space=pltpu.VMEM)
-    hbm = pl.BlockSpec(memory_space=pl.ANY)
+    smem = pl.BlockSpec(memory_space=pltpu.SMEM)
+    hbm = pl.BlockSpec(memory_space=pltpu.HBM)
     dma = pltpu.SemaphoreType.DMA
-    return pl.pallas_call(
+    results = pl.pallas_call(
         kernel,
         out_shape=(
             jax.ShapeDtypeStruct((seeds, hidden_width), BF16),
             jax.ShapeDtypeStruct((out_rows, hidden_width), F32),
             jax.ShapeDtypeStruct((out_rows, hidden_width), F32),
         ),
-        in_specs=[vmem] * 3 + [hbm] * 4,
+        in_specs=[vmem, smem] + [vmem] * 3 + [hbm] * 4,
         out_specs=(hbm, vmem, vmem),
         scratch_shapes=[
             pltpu.VMEM((node_count, width), BF16),
@@ -460,9 +472,12 @@
             pltpu.VMEM((width, hidden_width), BF16),
             pltpu.VMEM((seeds, hidden_width), BF16),
             pltpu.VMEM((seeds, node_count), BF16),
+            pltpu.VMEM((LANES, LANES), jnp.int32),
+            pltpu.VMEM((n, 1, LANES), jnp.int32),
             pltpu.VMEM((n, 1, LANES), jnp.int32),
             pltpu.VMEM((2, n // 2, per, width), BF16),
             pltpu.VMEM((4, LANES, width), BF16),
+            pltpu.VMEM((seeds, seeds), F32),
             pltpu.VMEM((seeds, seeds), BF16),
             pltpu.VMEM((2, seeds, LANES), BF16),
             pltpu.VMEM((nq, seeds, wq), F32),
@@ -492,18 +507,39 @@
             dma((nq, NC, NZ)),
         ],
         compiler_params=pltpu.CompilerParams(
-            collective_id=0, has_side_effects=True, vmem_limit_bytes=48 * 1024 * 1024
+            collective_id=0, has_side_effects=True, vmem_limit_bytes=62 * 1024 * 1024
         ),
         name="layer_step",
     )(
-        wanted,
-        ids,
-        tiles.reshape(-1, tiles.shape[3]),
+        block_counts,
+        tile_seed_block,
+        jnp.transpose(request_rows[0], (1, 2, 0)),
+        seed_rows.reshape(-1, LANES),
+        tiles[0],
         features,
         w_self,
         w_neigh,
         grad_out,
     )
+    return pl.pallas_call(
+        hand_out,
+        out_shape=tuple(jax.ShapeDtypeStruct(r.shape, r.dtype) for r in results),
+        in_specs=[hbm] * 3,
+        out_specs=(hbm,) * 3,
+        scratch_shapes=[dma((3,))],
+        name="hand_out",
+    )(*results)
+
+
+def hand_out(a_ref, b_ref, c_ref, a_out, b_out, c_out, sem):
+    copies = [
+        pltpu.make_async_copy(src, dst, sem.at[i])
+        for i, (src, dst) in enumerate(((a_ref, a_out), (b_ref, b_out), (c_ref, c_out)))
+    ]
+    for copy in copies:
+        copy.start()
+    for copy in copies:
+        copy.wait()
 
 
 def solution(mesh):

time: 58.7 us -> 77.8 us (1.33)
  Pallas kernels: 46.6 us -> 77 us
  local copies, waits for them, and re-layouts: 7.76 us -> 0 us
  other arithmetic: 3.36 us -> 0 us
    pallas_call x0 -> x1, Pallas kernels: none -> 28.9 us  [kernel_body(): pl.pallas_call(hand_out, out_shape=tuple((jax.ShapeDtypeStruct(r.shape, r...]
    unnamed x12 -> x0, local copies, waits for them, and re-layouts: 7.35 us -> none
    pallas_call x1, Pallas kernels: 46.6 us -> 48.1 us  [kernel_body(): pl.pallas_call(kernel, out_shape=(jax.ShapeDtypeStruct((seeds, hidden_wid...]
    unnamed x1 -> x0, other arithmetic: 1.32 us -> none
where the time goes in v2:
time: 77.8 us; the launch traced here: 77.6 us
  Pallas kernels  77 us (99%)
    pallas_call x1, Pallas kernels, kernel_body(): pl.pallas_call(kernel, out_shape=(jax.ShapeDtypeStruct((seeds, hidden_wid...  48.1 us
    pallas_call x1, Pallas kernels, kernel_body(): pl.pallas_call(hand_out, out_shape=tuple((jax.ShapeDtypeStruct(r.shape, r...  28.9 us

profile of v2, /device:TPU:0, one launch (start us, length us, event | category | flops | bytes accessed | tf_op | source)
XLA Modules:
  0.0 77.6 jit_solution(11633007396922083883)
XLA Ops:
  0.6 48.1 %layer_step.1 = (bf16[256,1024]{1,0:T(8,128)(2,1)}, f32[48,1024]{1,0:T(8,128)}, f32[48,1024]{1,0:T(8,128)}) custom-call(s32[1,16]{1,0:T(1,128)} %counts_ref.1, s32[1,32]{1,0:T(1,128)} %block_ref.1, s32[2,8,16]{2,1,0:T(8,128)} %bitcast.6, s32[2,128]{1,0:T(2,128)} %bitcast.7, bf16[32,8,128]{2,1,0:T(8,128)(2,1)} %bitcast.5, bf16[2048,768]{1,0:T(8,128)(2,1)} %feat_hbm.1, ...), custom_call_target="tpu_custom_call" | custom-call | tf_op jit(solution)/shard_map/layer_step/pallas_call | solution.py:460
  48.7 28.9 %hand_out.1 = (bf16[256,1024]{1,0:T(8,128)(2,1)}, f32[48,1024]{1,0:T(8,128)}, f32[48,1024]{1,0:T(8,128)}) custom-call(bf16[256,1024]{1,0:T(8,128)(2,1)} %get-tuple-element.6.a_ref, f32[48,1024]{1,0:T(8,128)} %get-tuple-element.7.b_ref, f32[48,1024]{1,0:T(8,128)} %get-tuple-element.8.c_ref), custom_call_target="tpu_custom_call" | custom-call | tf_op jit(solution)/shard_map/hand_out/pallas_call | solution.py:524

commit v3 on v2

--- a/solution.py
+++ b/solution.py
@@ -98,8 +98,8 @@
     wn_hbm,
     go_hbm,
     hid_hbm,
-    gs_ref,
-    gn_ref,
+    gs_hbm,
+    gn_hbm,
     feat,
     ws,
     wn,
@@ -115,8 +115,10 @@
     adjt,
     s,
     hid,
-    rrows,
-    at,
+    gs,
+    gn,
+    turned_rows,
+    recv_turned,
     bcat,
     bsend,
     xsend,
@@ -126,6 +128,7 @@
     zrecv,
     lsem,
     hsem,
+    osem,
     rq_s,
     rq_r,
     fr_s,
@@ -177,6 +180,18 @@
         req_ref[owner] = turned[owner : owner + 1, :]
     pl.semaphore_wait(barrier, n - 1)
 
+    chip_rows = width // (NZ * NX)
+
+    def put_turned(kind, h):
+        turned = rows[2 * kind + h].T
+        lanes = pl.ds(pl.multiple_of(h * LANES, LANES), LANES)
+        for zz in range(NZ):
+            for xx in range(NX):
+                start = (zz * NX + xx) * chip_rows
+                turned_rows[kind, xx, zz * chip_rows : (zz + 1) * chip_rows, lanes] = turned[
+                    start : start + chip_rows, :
+                ]
+
     ask = []
     for k, owner in enumerate(others):
         ask.append(
@@ -191,14 +206,6 @@
         )
         ask[-1].start()
     reqs[me] = req_ref[me]
-
-    for h in range(seeds // LANES):
-        put_one_hot(oh, down_rows(seeds_ref[h : h + 1, :]), h * LANES, node_count)
-    loads[0].wait()
-    for h in range(seeds // LANES):
-        rows[h] = jnp.dot(
-            oh[h * LANES : (h + 1) * LANES, :], feat[...], preferred_element_type=F32
-        ).astype(BF16)
 
     answer = []
     for step, h in enumerate((far, near)):
@@ -221,6 +228,8 @@
             jnp.broadcast_to(turned[0:per, j : j + 1], (per, LANES)) for j in range(half_n)
         ]
         put_one_hot(oh, jnp.concatenate(wanted, axis=0), 0, node_count)
+        if step == 0:
+            loads[0].wait()
         ans[h] = (
             jnp.dot(oh[0:LANES, :], feat[...], preferred_element_type=F32)
             .astype(BF16)
@@ -245,6 +254,13 @@
             copy.start()
             answer.append(copy)
 
+    for h in range(seeds // LANES):
+        put_one_hot(oh, down_rows(seeds_ref[h : h + 1, :]), h * LANES, node_count)
+    for h in range(seeds // LANES):
+        rows[h] = jnp.dot(
+            oh[h * LANES : (h + 1) * LANES, :], feat[...], preferred_element_type=F32
+        ).astype(BF16)
+
     for slot in range(tiles_ref.shape[0]):
         tile = tiles_ref[slot].astype(F32)
         for b in range(seeds // LANES):
@@ -281,19 +297,23 @@
             else:
                 wait()
 
+    put_turned(0, 0)
+    put_turned(0, 1)
     own.wait()
     wait_rows(near, True)
+    put_turned(1, near)
     for q in range(nq):
         msg = jnp.dot(
             rows[2 + near], wn[:, q * wq : (q + 1) * wq], preferred_element_type=F32
         ).astype(BF16)
         s[q] += jnp.dot(adjt[near], msg, preferred_element_type=F32)
     wait_rows(far, False)
+    put_turned(1, far)
 
     sibling = dev(z, x, 1 - core)
     trade_a = pltpu.make_async_remote_copy(
-        src_ref=rows.at[pl.ds(2 * (1 - core), 2)],
-        dst_ref=rrows,
+        src_ref=turned_rows.at[1 - core],
+        dst_ref=recv_turned,
         send_sem=a_s,
         recv_sem=a_r,
         device_id=sibling,
@@ -339,27 +359,18 @@
         write.start()
         writes.append(write)
 
-    chip_rows = width // (NZ * NX)
-
-    def put_transposed(values, at_col):
-        turned = values.T
-        for zz in range(NZ):
-            for xx in range(NX):
-                start = (zz * NX + xx) * chip_rows
-                at[xx, zz * chip_rows : (zz + 1) * chip_rows, at_col : at_col + seeds] = turned[
-                    start : start + chip_rows, :
-                ]
-
     peer = dev(z, 1 - x, core)
+
+    def chip_sum(q, half):
+        return (
+            jnp.dot(turned_rows[core, half], bcat[q, 0:seeds, :], preferred_element_type=F32)
+            + jnp.dot(recv_turned[half], bcat[q, seeds : 2 * seeds, :], preferred_element_type=F32)
+        ).reshape(NZ, chip_rows, wq)
 
     def x_part(q):
         trade_b[q].wait_recv()
-        xsend[q] = (
-            jnp.dot(at[1 - x], bcat[q], preferred_element_type=F32)
-            .astype(BF16)
-            .reshape(NZ, chip_rows, wq)
-        )
-        for k in range(NZ - 1, -1, -1):
+        xsend[q] = chip_sum(q, 1 - x).astype(BF16)
+        for k in (2, 1, 3, 0):
             zb = z_xor(k)
             copy = pltpu.make_async_remote_copy(
                 src_ref=xsend.at[q, zb],
@@ -371,12 +382,12 @@
             )
             copy.start()
             xcopies.append(copy)
-        gk[q] = jnp.dot(at[x], bcat[q], preferred_element_type=F32).reshape(NZ, chip_rows, wq)
+        gk[q] = chip_sum(q, x)
 
     def z_part(q):
-        for k in range(NZ - 1, -1, -1):
+        for k in (2, 1, 3, 0):
             zb = z_xor(k)
-            xcopies[q * NZ + NZ - 1 - k].wait_recv()
+            xcopies[q * NZ + (2, 1, 3, 0).index(k)].wait_recv()
             total = gk[q, zb] + xrecv[q, zb].astype(F32)
             zsend[q, zb] = total.astype(BF16).reshape(NC, chip_rows // NC, wq)
             for i in range(NC):
@@ -410,22 +421,25 @@
                     device_id=sibling,
                     device_id_type=MESH,
                 ).wait_recv()
-        for g, out in enumerate((gs_ref, gn_ref)):
+        for g, (out, out_hbm) in enumerate(((gs, gs_hbm), (gn, gn_hbm))):
             parts = zrecv[q, g].astype(F32)
-            out[:, q * wq : (q + 1) * wq] = (parts[0] + parts[1]) + (parts[2] + parts[3])
+            out[q] = (parts[0] + parts[1]) + (parts[2] + parts[3])
+            write = pltpu.make_async_copy(
+                out.at[q], out_hbm.at[:, pl.ds(q * wq, wq)], osem.at[q, g]
+            )
+            write.start()
+            writes.append(write)
 
     seed_part(0)
-    put_transposed(rows[pl.ds(2 * core, 2)].reshape(seeds, width), 0)
-    seed_part(1)
     trade_a.wait_recv()
-    put_transposed(rrows[...].reshape(seeds, width), seeds)
     x_part(0)
-    for q in range(2, nq):
+    for q in range(1, nq):
         seed_part(q)
-        x_part(q - 1)
-    x_part(nq - 1)
+    x_part(1)
     for q in range(nq):
         z_part(q)
+        if q + 2 < nq:
+            x_part(q + 2)
     for q in range(nq):
         last_part(q)
     for copy in ask + answer + [trade_a] + trade_b + xcopies + zcopies:
@@ -465,7 +479,7 @@
             jax.ShapeDtypeStruct((out_rows, hidden_width), F32),
         ),
         in_specs=[vmem, smem] + [vmem] * 3 + [hbm] * 4,
-        out_specs=(hbm, vmem, vmem),
+        out_specs=(hbm,) * 3,
         scratch_shapes=[
             pltpu.VMEM((node_count, width), BF16),
             pltpu.VMEM((width, hidden_width), BF16),
@@ -482,8 +496,10 @@
             pltpu.VMEM((2, seeds, LANES), BF16),
             pltpu.VMEM((nq, seeds, wq), F32),
             pltpu.VMEM((nq, seeds, wq), BF16),
-            pltpu.VMEM((2, LANES, width), BF16),
-            pltpu.VMEM((NX, NZ * chip_rows, 2 * seeds), BF16),
+            pltpu.VMEM((nq, out_rows, wq), F32),
+            pltpu.VMEM((nq, out_rows, wq), F32),
+            pltpu.VMEM((2, NX, NZ * chip_rows, seeds), BF16),
+            pltpu.VMEM((NX, NZ * chip_rows, seeds), BF16),
             pltpu.VMEM((nq, 2 * seeds, wq), BF16),
             pltpu.VMEM((nq, seeds, wq), BF16),
             pltpu.VMEM((nq, NZ, chip_rows, wq), BF16),
@@ -493,6 +509,7 @@
             pltpu.VMEM((nq, NC, NZ, out_rows, wq), BF16),
             dma((4,)),
             dma((nq + 1,)),
+            dma((nq, NC)),
             dma((n - 1,)),
             dma((n,)),
             dma((2, n // 2)),
@@ -526,20 +543,29 @@
         out_shape=tuple(jax.ShapeDtypeStruct(r.shape, r.dtype) for r in results),
         in_specs=[hbm] * 3,
         out_specs=(hbm,) * 3,
-        scratch_shapes=[dma((3,))],
+        scratch_shapes=[pltpu.VMEM(r.shape, r.dtype) for r in results] + [dma((2, 4))],
+        compiler_params=pltpu.CompilerParams(vmem_limit_bytes=62 * 1024 * 1024),
         name="hand_out",
     )(*results)
 
 
-def hand_out(a_ref, b_ref, c_ref, a_out, b_out, c_out, sem):
-    copies = [
-        pltpu.make_async_copy(src, dst, sem.at[i])
-        for i, (src, dst) in enumerate(((a_ref, a_out), (b_ref, b_out), (c_ref, c_out)))
+def hand_out(a_ref, b_ref, c_ref, a_out, b_out, c_out, a_mid, b_mid, c_mid, sem):
+    half = a_ref.shape[0] // 2
+    stages = ((b_ref, b_mid, b_out), (c_ref, c_mid, c_out)) + tuple(
+        tuple(r.at[pl.ds(i * half, half)] for r in (a_ref, a_mid, a_out)) for i in range(2)
+    )
+    fetches = [
+        pltpu.make_async_copy(src, mid, sem.at[0, i]) for i, (src, mid, _) in enumerate(stages)
     ]
-    for copy in copies:
-        copy.start()
-    for copy in copies:
-        copy.wait()
+    for fetch in fetches:
+        fetch.start()
+    stores = []
+    for i, (_, mid, out) in enumerate(stages):
+        fetches[i].wait()
+        stores.append(pltpu.make_async_copy(mid, out, sem.at[1, i]))
+        stores[-1].start()
+    for store in stores:
+        store.wait()
 
 
 def solution(mesh):

time: 77.8 us -> 50.4 us (0.65)
  Pallas kernels: 77 us -> 49.6 us
    pallas_call x1, Pallas kernels: 28.9 us -> 2.01 us  [kernel_body(): pl.pallas_call(hand_out, out_shape=tuple((jax.ShapeDtypeStruct(r.shape, r...]
where the time goes in v3:
time: 50.4 us; the launch traced here: 50.2 us
  Pallas kernels  49.6 us (98%)
  between operations  0.64 us (1%)
    pallas_call x1, Pallas kernels, kernel_body(): pl.pallas_call(kernel, out_shape=(jax.ShapeDtypeStruct((seeds, hidden_wid...  47.6 us
    pallas_call x1, Pallas kernels, kernel_body(): pl.pallas_call(hand_out, out_shape=tuple((jax.ShapeDtypeStruct(r.shape, r...  2.01 us

profile of v3, /device:TPU:0, one launch (start us, length us, event | category | flops | bytes accessed | tf_op | source)
XLA Modules:
  0.0 50.2 jit_solution(5572411389511603359)
XLA Ops:
  0.6 47.6 %layer_step.1 = (bf16[256,1024]{1,0:T(8,128)(2,1)}, f32[48,1024]{1,0:T(8,128)}, f32[48,1024]{1,0:T(8,128)}) custom-call(s32[1,16]{1,0:T(1,128)} %counts_ref.1, s32[1,32]{1,0:T(1,128)} %block_ref.1, s32[2,8,16]{2,1,0:T(8,128)} %bitcast.6, s32[2,128]{1,0:T(2,128)} %bitcast.7, bf16[32,8,128]{2,1,0:T(8,128)(2,1)} %bitcast.5, bf16[2048,768]{1,0:T(8,128)(2,1)} %feat_hbm.1, ...), custom_call_target="tpu_custom_call" | custom-call | tf_op jit(solution)/shard_map/layer_step/pallas_call | solution.py:474
  48.2 2.0 %hand_out.1 = (bf16[256,1024]{1,0:T(8,128)(2,1)}, f32[48,1024]{1,0:T(8,128)}, f32[48,1024]{1,0:T(8,128)}) custom-call(bf16[256,1024]{1,0:T(8,128)(2,1)} %get-tuple-element.6.a_ref, f32[48,1024]{1,0:T(8,128)} %get-tuple-element.7.b_ref, f32[48,1024]{1,0:T(8,128)} %get-tuple-element.8.c_ref), custom_call_target="tpu_custom_call" | custom-call | tf_op jit(solution)/shard_map/hand_out/pallas_call | solution.py:541

commit v4 on v3

--- a/solution.py
+++ b/solution.py
@@ -12,6 +12,7 @@
 F32 = jnp.float32
 LANES = 128
 NZ, NX, NC = 4, 2, 2
+ORDER = (3, 1, 2, 0)
 
 
 def activate(values):
@@ -125,6 +126,7 @@
     xrecv,
     gk,
     zsend,
+    zmid,
     zrecv,
     lsem,
     hsem,
@@ -370,7 +372,7 @@
     def x_part(q):
         trade_b[q].wait_recv()
         xsend[q] = chip_sum(q, 1 - x).astype(BF16)
-        for k in (2, 1, 3, 0):
+        for k in ORDER:
             zb = z_xor(k)
             copy = pltpu.make_async_remote_copy(
                 src_ref=xsend.at[q, zb],
@@ -384,46 +386,79 @@
             xcopies.append(copy)
         gk[q] = chip_sum(q, x)
 
-    def z_part(q):
-        for k in (2, 1, 3, 0):
+    def piece(q, k):
+        zb = z_xor(k)
+        xcopies[q * NZ + ORDER.index(k)].wait_recv()
+        return (gk[q, zb] + xrecv[q, zb].astype(F32)).reshape(NC, chip_rows // NC, wq)
+
+    def z_send(src, dst, send_sem, recv_sem, device):
+        copy = pltpu.make_async_remote_copy(
+            src_ref=src,
+            dst_ref=dst,
+            send_sem=send_sem,
+            recv_sem=recv_sem,
+            device_id=device,
+            device_id_type=MESH,
+        )
+        copy.start()
+        zcopies.append(copy)
+        return copy
+
+    pairs = []
+
+    def z_pair(q):
+        for i, k in ((1, 3), (0, 1)):
             zb = z_xor(k)
-            xcopies[q * NZ + (2, 1, 3, 0).index(k)].wait_recv()
-            total = gk[q, zb] + xrecv[q, zb].astype(F32)
-            zsend[q, zb] = total.astype(BF16).reshape(NC, chip_rows // NC, wq)
-            for i in range(NC):
-                cc = 1 - core if i == 0 else core
-                if k == 0 and i == 1:
-                    zrecv[q, core, z] = zsend[q, z, core]
-                    continue
-                copy = pltpu.make_async_remote_copy(
-                    src_ref=zsend.at[q, zb, cc],
-                    dst_ref=zrecv.at[q, core, z],
-                    send_sem=z_s.at[q, k, i],
-                    recv_sem=z_r.at[q, core, z],
-                    device_id=dev(zb, x, cc),
-                    device_id_type=MESH,
+            zsend[q, zb] = piece(q, k).astype(BF16)
+            pairs.append(
+                z_send(
+                    zsend.at[q, zb],
+                    zmid.at[q, i],
+                    z_s.at[q, 0, i],
+                    z_r.at[q, i, 2],
+                    dev(z_xor(1), x, core),
                 )
-                copy.start()
-                zcopies.append(copy)
+            )
+
+    def z_cross(q):
+        across = z_xor(2)
+        total = piece(q, 2)
+        pairs[2 * q].wait_recv()
+        zsend[q, across] = (total + zmid[q, 1].astype(F32)).astype(BF16)
+        for cc in range(NC):
+            z_send(
+                zsend.at[q, across, cc],
+                zrecv.at[q, core, 0],
+                z_s.at[q, 1, cc],
+                z_r.at[q, core, 0],
+                dev(across, x, cc),
+            )
+        total = piece(q, 0)
+        pairs[2 * q + 1].wait_recv()
+        zsend[q, z] = (total + zmid[q, 0].astype(F32)).astype(BF16)
+        z_send(
+            zsend.at[q, z, 1 - core],
+            zrecv.at[q, core, 1],
+            z_s.at[q, 2, 0],
+            z_r.at[q, core, 1],
+            sibling,
+        )
+        zrecv[q, core, 1] = zsend[q, z, core]
 
     def last_part(q):
-        for i in range(NC):
-            for k in range(NZ):
-                if i == 0 and k == 0:
-                    continue
-                g = core if i == 0 else 1 - core
-                where = zrecv.at[q, g, z_xor(k)]
-                pltpu.make_async_remote_copy(
-                    src_ref=where,
-                    dst_ref=where,
-                    send_sem=z_s.at[0, 0, 0],
-                    recv_sem=z_r.at[q, g, z_xor(k)],
-                    device_id=sibling,
-                    device_id_type=MESH,
-                ).wait_recv()
+        for g, i in ((1 - core, 1), (0, 0), (1, 0)):
+            where = zrecv.at[q, g, i]
+            pltpu.make_async_remote_copy(
+                src_ref=where,
+                dst_ref=where,
+                send_sem=z_s.at[0, 0, 0],
+                recv_sem=z_r.at[q, g, i],
+                device_id=sibling,
+                device_id_type=MESH,
+            ).wait_recv()
         for g, (out, out_hbm) in enumerate(((gs, gs_hbm), (gn, gn_hbm))):
             parts = zrecv[q, g].astype(F32)
-            out[q] = (parts[0] + parts[1]) + (parts[2] + parts[3])
+            out[q] = parts[0] + parts[1]
             write = pltpu.make_async_copy(
                 out.at[q], out_hbm.at[:, pl.ds(q * wq, wq)], osem.at[q, g]
             )
@@ -437,9 +472,10 @@
         seed_part(q)
     x_part(1)
     for q in range(nq):
-        z_part(q)
+        z_pair(q)
         if q + 2 < nq:
             x_part(q + 2)
+        z_cross(q)
     for q in range(nq):
         last_part(q)
     for copy in ask + answer + [trade_a] + trade_b + xcopies + zcopies:
@@ -506,7 +542,8 @@
             pltpu.VMEM((nq, NZ, chip_rows, wq), BF16),
             pltpu.VMEM((nq, NZ, chip_rows, wq), F32),
             pltpu.VMEM((nq, NZ, NC, out_rows, wq), BF16),
-            pltpu.VMEM((nq, NC, NZ, out_rows, wq), BF16),
+            pltpu.VMEM((nq, 2, NC, out_rows, wq), BF16),
+            pltpu.VMEM((nq, NC, 2, out_rows, wq), BF16),
             dma((4,)),
             dma((nq + 1,)),
             dma((nq, NC)),
@@ -521,7 +558,7 @@
             dma((nq, NZ)),
             dma((nq, NZ)),
             dma((nq, NZ, NC)),
-            dma((nq, NC, NZ)),
+            dma((nq, NC, 3)),
         ],
         compiler_params=pltpu.CompilerParams(
             collective_id=0, has_side_effects=True, vmem_limit_bytes=62 * 1024 * 1024

time: 50.4 us -> 50.4 us (level)
  no operation moved by 1% of the time
where the time goes in v4:
time: 50.4 us; the launch traced here: 50.2 us
  Pallas kernels  49.6 us (98%)
  between operations  0.64 us (1%)
    pallas_call x1, Pallas kernels, kernel_body(): pl.pallas_call(kernel, out_shape=(jax.ShapeDtypeStruct((seeds, hidden_wid...  47.6 us
    pallas_call x1, Pallas kernels, kernel_body(): pl.pallas_call(hand_out, out_shape=tuple((jax.ShapeDtypeStruct(r.shape, r...  2.01 us

profile of v4, /device:TPU:0, one launch (start us, length us, event | category | flops | bytes accessed | tf_op | source)
XLA Modules:
  0.0 50.2 jit_solution(1863505267838121303)
XLA Ops:
  0.6 47.6 %layer_step.1 = (bf16[256,1024]{1,0:T(8,128)(2,1)}, f32[48,1024]{1,0:T(8,128)}, f32[48,1024]{1,0:T(8,128)}) custom-call(s32[1,16]{1,0:T(1,128)} %counts_ref.1, s32[1,32]{1,0:T(1,128)} %block_ref.1, s32[2,8,16]{2,1,0:T(8,128)} %bitcast.6, s32[2,128]{1,0:T(2,128)} %bitcast.7, bf16[32,8,128]{2,1,0:T(8,128)(2,1)} %bitcast.5, bf16[2048,768]{1,0:T(8,128)(2,1)} %feat_hbm.1, ...), custom_call_target="tpu_custom_call" | custom-call | tf_op jit(solution)/shard_map/layer_step/pallas_call | solution.py:510
  48.2 2.0 %hand_out.1 = (bf16[256,1024]{1,0:T(8,128)(2,1)}, f32[48,1024]{1,0:T(8,128)}, f32[48,1024]{1,0:T(8,128)}) custom-call(bf16[256,1024]{1,0:T(8,128)(2,1)} %get-tuple-element.6.a_ref, f32[48,1024]{1,0:T(8,128)} %get-tuple-element.7.b_ref, f32[48,1024]{1,0:T(8,128)} %get-tuple-element.8.c_ref), custom_call_target="tpu_custom_call" | custom-call | tf_op jit(solution)/shard_map/hand_out/pallas_call | solution.py:578
